TPU v7x, 512 devices: a whole 4x4x16 slice. The times are simulated.
512 devices in a mesh: var: 128 (over x, z, core), samp: 4 (over y).
Axes of the slice: x: 4, y: 4, z: 16, core: 2. Of those that a mesh axis runs over, the one named last changes fastest.
Arguments:
- data: bfloat16 [128, 131072], P('samp', 'var'), may hold values from -6 to 6
- omega: float32 [8192, 128, 128], P(('var', 'samp')), may hold values from -0.3 to 2.3, as said below
- tile_row: int32 [128, 64], P('var'), may hold values from 0 to 7, as said below
- tile_col: int32 [128, 64], P('var'), may hold values from 0 to 1023, as said below
- tile_count: int32 [128], P('var'), may hold values from 60 to 64, as said below
- tile_active: int32 [128, 64], P('var'), may hold values 0 or 1
Outputs:
- omega_next: float32 [8192, 128, 128], P(('var', 'samp'))
Inputs may be any that keep to these rules, and one draw needn't show every extreme that they name: `tile_row`: entries 0 to 7 of a block row have tile rows 0 to 7 in order; the others name any tile row of the block row. `tile_col`: entry k < 8 of block row r is column tile r * 8 + k. Every other entry names a column tile of another block row; no column tile twice in a block row, and at most 1 column tiles from any one other block row, a bound that some block row reaches. `tile_count`: some block row lists all 64 entries. `omega`: on entries k < 8 the diagonal of each tile lies between 0.7 and 2.3.
All inputs are finite; a program needn't handle non-finite values. No bound on the sum of `tile_active` on one device may be relied on, other than what follows from the above.
Results may differ from a plain program's by a relative error of at most 0.02.
Values may be sent and summed in bfloat16 or wider, within the bound.
A program may use at most 128 MiB of HBM per device.

v0:
```python
import jax
import jax.numpy as jnp
from jax import lax
from jax.sharding import PartitionSpec as P

step_size = 1.0
penalty = 0.05


def request_table(columns, count, owners, slot_cap, row_tiles):
    entry_count = columns.shape[0]
    entries = jnp.arange(entry_count, dtype=jnp.int32)
    remote = (entries >= row_tiles) & (entries < count)
    peer_owner = columns // row_tiles
    local_tile = columns % row_tiles
    earlier = (
        (peer_owner[:, None] == peer_owner[None, :])
        & remote[None, :]
        & (entries[None, :] < entries[:, None])
    )
    peer_rank = jnp.sum(earlier.astype(jnp.int32), axis=1)
    slot_index = jnp.where(remote, peer_owner * slot_cap + peer_rank, 0)
    slot_range = jnp.arange(owners * slot_cap, dtype=jnp.int32)
    matched = (slot_index[:, None] == slot_range[None, :]) & remote[:, None]
    table = jnp.sum(jnp.where(matched, (local_tile + 1)[:, None], 0), axis=0)
    return (table.reshape(owners, slot_cap), slot_index, remote)


def pick_tiles(source_tiles, wanted):
    row_tiles = source_tiles.shape[1]
    selector = (
        wanted[:, :, None] == jnp.arange(1, row_tiles + 1, dtype=jnp.int32)[None, None, :]
    ).astype(jnp.bfloat16)
    picked = jnp.einsum("qcr,srt->sqct", selector, source_tiles, preferred_element_type=jnp.float32)
    return picked.astype(jnp.bfloat16)


def place_tiles(incoming, slot_index, remote, own_tiles, local_index):
    sample_count, owners, slot_cap, tile_size = incoming.shape
    flat_slots = incoming.reshape(sample_count, owners * slot_cap, tile_size)
    fetched = jnp.take(flat_slots, slot_index, axis=1)
    own_part = jnp.take(own_tiles, local_index, axis=1)
    return jnp.where(remote[None, :, None], fetched, own_part)


def local(data, omega, tile_row, tile_col, tile_count, tile_active):
    sample_count, block_width = data.shape
    share_count = omega.shape[0]
    tile_size = omega.shape[1]
    row_tiles = block_width // tile_size
    entry_count = tile_col.shape[1]
    owners = lax.axis_size("var")
    slot_cap = (entry_count - row_tiles + owners - 2) // (owners - 1)
    owner_self = lax.axis_index("var")
    samp_self = lax.axis_index("samp")
    columns = tile_col[0]
    rows_here = tile_row[0]
    count = tile_count[0]
    entries = jnp.arange(entry_count, dtype=jnp.int32)
    is_live = entries < count
    data_tiles = data.reshape(sample_count, row_tiles, tile_size)
    own_table, slot_index, remote = request_table(columns, count, owners, slot_cap, row_tiles)
    local_index = jnp.where(remote, 0, jnp.clip(columns - owner_self * row_tiles, 0, row_tiles - 1))
    wanted = lax.all_to_all(own_table, "var", split_axis=0, concat_axis=0, tiled=True)
    incoming = lax.all_to_all(
        pick_tiles(data_tiles, wanted), "var", split_axis=1, concat_axis=1, tiled=True
    )
    col_data = place_tiles(incoming, slot_index, remote, data_tiles, local_index)
    omega_low = omega.astype(jnp.bfloat16)
    products = jnp.einsum(
        "skt,kut->sku",
        col_data,
        lax.all_gather(omega_low, "samp", axis=0, tiled=True),
        preferred_element_type=jnp.float32,
    )
    weights = (
        (rows_here[:, None] == jnp.arange(row_tiles, dtype=jnp.int32)[None, :]) & is_live[:, None]
    ).astype(jnp.float32)
    image = jnp.einsum("sku,kr->sru", products, weights).astype(jnp.bfloat16)
    incoming_image = lax.all_to_all(
        pick_tiles(image, wanted), "var", split_axis=1, concat_axis=1, tiled=True
    )
    col_image = place_tiles(incoming_image, slot_index, remote, image, local_index)
    row_data = jnp.take(data_tiles, rows_here, axis=1)
    row_image = jnp.take(image, rows_here, axis=1)
    scale = 0.5 / (sample_count * lax.axis_size("samp"))
    first = jnp.einsum("sku,skt->kut", row_image, col_data, preferred_element_type=jnp.float32)
    second = jnp.einsum("sku,skt->kut", row_data, col_image, preferred_element_type=jnp.float32)
    gradient = lax.psum_scatter(
        ((first + second) * scale).astype(jnp.bfloat16), "samp", scatter_dimension=0, tiled=True
    ).astype(jnp.float32)
    share_entries = samp_self * share_count + jnp.arange(share_count, dtype=jnp.int32)
    share_live = share_entries < count
    share_diag = share_entries < row_tiles
    share_active = jnp.take(tile_active[0], share_entries)
    identity = jnp.eye(tile_size, dtype=jnp.float32)
    diagonal = jnp.diagonal(omega, axis1=1, axis2=2)
    safe_diag = jnp.where(share_diag[:, None], diagonal, 1.0)
    gradient = gradient - jnp.where(
        share_diag[:, None, None], identity[None, :, :] / safe_diag[:, None, :], 0.0
    )
    stepped = omega - step_size * gradient
    shrunk = jnp.sign(stepped) * jnp.maximum(jnp.abs(stepped) - step_size * penalty, 0.0)
    on_diag = share_diag[:, None, None] & (identity[None, :, :] > 0.5)
    proximal = jnp.where(on_diag, stepped, shrunk)
    held = jnp.where(share_active[:, None, None] > 0, proximal, omega)
    return jnp.where(share_live[:, None, None], held, 0.0)


def solution(mesh):
    placed = (
        P("samp", "var"),
        P(("var", "samp"), None, None),
        P("var", None),
        P("var", None),
        P("var"),
        P("var", None),
    )
    return jax.shard_map(
        local, mesh=mesh, in_specs=placed, out_specs=P(("var", "samp"), None, None), check_vma=False
    )
```

profile of v0, /device:TPU:1, one launch (start us, length us, event | category | flops | bytes accessed | tf_op | source)
XLA Modules:
  0.0 226.0 jit_solution(3204313692680687741)
XLA Ops:
  6.5 0.0 copy-start
  6.5 0.0 copy-start.4
  6.5 0.0 copy-start.2
  6.5 0.0 copy-start.1
  6.5 0.8 and_select_fusion.2
  7.3 0.7 fusion.41
  8.6 0.2 convert_reduce_fusion
  8.8 0.1 select_reduce_fusion
  8.9 0.7 copy.48
  9.7 20.4 %all-to-all-start = ((s32[128,1,1]{2,1,0:T(1,128)}), s32[128,1,1]{2,1,0:T(1,128)S(1)}, u32[]{:S(2)}, u32[]{:S(2)}) async-start(s32[128,1,1]{2,1,0:T(1,128)} %copy.48), calls=%async_computation | async-start | bytes 131072 | tf_op jit(solution)/shard_map/all_to_all | solution.py:64
  30.1 0.9 copy.59
  31.0 14.1 %all-to-all-done = s32[128,1,1]{2,1,0:T(1,128)S(1)} async-done(((s32[128,1,1]{2,1,0:T(1,128)}), s32[128,1,1]{2,1,0:T(1,128)S(1)}, u32[]{:S(2)}, u32[]{:S(2)}) %all-to-all-start) | async-done | bytes 544 | tf_op jit(solution)/shard_map/all_to_all | solution.py:64
  45.1 2.3 %reduce = s32[128]{0:T(128)S(1)} reduce(s32[128,1,1]{2,1,0:T(1,128)S(1)} %all-to-all-done, s32[]{:T(128)} %constant.56.clone.1), dimensions={1,2}, to_apply=%all_to_all.15.reduce_sub_computation | reduce | bytes 1028 | tf_op jit(solution)/shard_map/all_to_all | solution.py:64
  47.4 0.6 fusion
  48.0 1.6 copy.49
  49.6 6.6 %all-to-all-start.1 = ((bf16[32,128,1,128]{3,0,2,1:T(8,128)(2,1)}), bf16[32,128,1,128]{3,0,2,1:T(8,128)(2,1)S(1)}, u32[]{:S(2)}, u32[]{:S(2)}) async-start(bf16[32,128,1,128]{3,0,2,1:T(8,128)(2,1)} %copy.49), calls=%async_computation.1 | async-start | bytes 2097152 | tf_op jit(solution)/shard_map/all_to_all | solution.py:65
  56.2 0.0 copy-start.3
  56.2 0.0 all-gather.2.cloned.1.call-start
  56.3 0.0 copy-done.1
  56.3 0.9 convert_element_type.60
  57.2 0.0 all-gather.2.cloned.1.call-update
  57.2 0.0 copy-done.4
  57.3 0.0 copy-done.2
  57.3 0.7 gather_fusion.3
  58.0 52.7 %all-to-all-done.1 = bf16[32,128,1,128]{3,0,2,1:T(8,128)(2,1)S(1)} async-done(((bf16[32,128,1,128]{3,0,2,1:T(8,128)(2,1)}), bf16[32,128,1,128]{3,0,2,1:T(8,128)(2,1)S(1)}, u32[]{:S(2)}, u32[]{:S(2)}) %all-to-all-start.1) | async-done | bytes 1048608 | tf_op jit(solution)/shard_map/all_to_all | solution.py:65
  110.7 0.7 gather_fusion.2
  111.3 0.0 all-gather.2.cloned.1.call-done
  111.4 2.8 %convolution_bitcast_fusion = bf16[32,64,128]{2,0,1:T(8,128)(2,1)S(1)} fusion(bf16[64,128,128]{2,1,0:T(8,128)(2,1)} %all-gather.2.cloned.1.call-done, bf16[64,32,128]{2,1,0:T(8,128)(2,1)S(1)} %gather_fusion.3, bf16[64,32,128]{2,1,0:T(8,128)(2,1)S(1)} %gather_fusion.2, pred[64]{0:T(512)(128)(4,1)S(1)} %get-tuple-element.9, ...), kind=kOutput, calls=%fused_computation.11 | convolution fusion | flops 67895296 | bytes 3670208 | tf_op jit(solution)/shard_map/skt,kut->sku/dot_general | solution.py:70
  114.2 0.0 copy-done.3
  114.2 0.3 fusion.2
  114.5 0.6 fusion.1
  115.0 1.7 copy.54
  116.7 8.5 %all-to-all-start.2 = ((bf16[32,128,1,128]{3,0,2,1:T(8,128)(2,1)}), bf16[32,128,1,128]{3,0,2,1:T(8,128)(2,1)S(1)}, u32[]{:S(2)}, u32[]{:S(2)}) async-start(bf16[32,128,1,128]{3,0,2,1:T(8,128)(2,1)} %copy.54), calls=%async_computation.2 | async-start | bytes 2097152 | tf_op jit(solution)/shard_map/all_to_all | solution.py:80
  125.2 0.2 reduce-scatter.2.cloned.1.call-start
  125.5 1.4 gather_fusion.5
  126.9 1.5 gather_fusion.4
  128.4 1.4 gather_fusion.7
  129.8 4.0 %fusion.8 = f32[64,128,128]{2,1,0:T(8,128)} fusion(bf16[64,32,128]{2,1,0:T(8,128)(2,1)} %gather_fusion.4, pred[64]{0:T(512)(128)(4,1)S(1)} %compare_and_fusion, bf16[64,32,128]{2,1,0:T(8,128)(2,1)S(1)} %gather_fusion.3, bf16[64,32,128]{2,1,0:T(8,128)(2,1)S(1)} %gather_fusion.2, pred[64]{0:T(512)(128)(4,1)S(1)} %get-tuple-element.9, ...), kind=kOutput, calls=%fused_computation.24 | convolution fusion | flops 68157440 | bytes 5767424 | tf_op jit(solution)/shard_map/sku,skt->kut/dot_general | solution.py:87
  133.8 45.7 %all-to-all-done.2 = bf16[32,128,1,128]{3,0,2,1:T(8,128)(2,1)S(1)} async-done(((bf16[32,128,1,128]{3,0,2,1:T(8,128)(2,1)}), bf16[32,128,1,128]{3,0,2,1:T(8,128)(2,1)S(1)}, u32[]{:S(2)}, u32[]{:S(2)}) %all-to-all-start.2) | async-done | bytes 1048608 | tf_op jit(solution)/shard_map/all_to_all | solution.py:80
  179.6 0.7 gather_fusion.6
  180.2 5.0 %multiply_convert_fusion = bf16[64,128,128]{2,1,0:T(8,128)(2,1)} fusion(f32[64,128,128]{2,1,0:T(8,128)} %fusion.8, bf16[64,32,128]{2,1,0:T(8,128)(2,1)} %gather_fusion.7, bf16[64,32,128]{2,1,0:T(8,128)(2,1)S(1)} %gather_fusion.6, bf16[64,32,128]{2,1,0:T(8,128)(2,1)} %gather_fusion.5, pred[64]{0:T(512)(128)(4,1)S(1)} %compare_and_fusion, ...), kind=kOutput, calls=%fused_computation.8 | convolution fusion | flops 71303168 | bytes 7864576 | tf_op jit(solution)/shard_map/sku,skt->kut/dot_general | solution.py:88
  185.3 0.0 reduce-scatter.2.cloned.1.call-update
  185.3 4.6 %copy.56 = f32[16,128,128]{0,2,1:T(8,128)} copy(f32[16,128,128]{2,1,0:T(8,128)S(1)} %copy-done.1) | data formatting | bytes 2097152 | tf_op args[1]
  189.9 1.8 gather_fusion.1
  191.7 0.1 copy.57
  191.8 0.0 copy-done
  191.8 0.7 gather_fusion
  192.5 23.8 %reduce-scatter.2.cloned.1.call-done = bf16[16,128,128]{2,1,0:T(8,128)(2,1)} async-done(((bf16[64,128,128]{2,1,0:T(8,128)(2,1)}), bf16[16,128,128]{2,1,0:T(8,128)(2,1)}) %reduce-scatter.2.cloned.1.call-update) | async-done | bytes 524304 | tf_op jit(solution)/shard_map/reduce_scatter | solution.py:89
  216.3 2.9 %select_select_fusion = f32[16,128,128]{2,1,0:T(8,128)} fusion(f32[16,128,128]{2,1,0:T(8,128)S(1)} %copy-done.1, bf16[16,128,128]{2,1,0:T(8,128)(2,1)} %reduce-scatter.2.cloned.1.call-done, f32[16,128]{1,0:T(8,128)S(1)} %copy.57, f32[128,128]{1,0:T(8,128)S(1)} %get-tuple-element.15, pred[16]{0:T(512)(128)(4,1)S(1)} %fusion.44, ...), kind=kLoop, calls=%fused_computation.20 | loop fusion | flops 3670016 | bytes 2711600 | tf_op jit(solution)/shard_map/jit(_where)/select_n | solution.py:107
  (20 shorter events, 0.2 us)
Async XLA Ops:
  6.5 185.3 %copy-start = (s32[1,64]{1,0:T(1,128)S(1)}, s32[1,64]{1,0:T(1,128)}, u32[]{:S(2)}) copy-start(s32[1,64]{1,0:T(1,128)} %param.15) | copy-start | bytes 772
  6.5 50.7 %copy-start.4 = (s32[1,64]{1,0:T(1,128)S(1)}, s32[1,64]{1,0:T(1,128)}, u32[]{:S(2)}) copy-start(s32[1,64]{1,0:T(1,128)} %param.13) | copy-start | bytes 772
  6.5 50.7 %copy-start.2 = (bf16[32,1024]{1,0:T(8,128)(2,1)S(1)}, bf16[32,1024]{1,0:T(8,128)(2,1)}, u32[]{:S(2)}) copy-start(bf16[32,1024]{1,0:T(8,128)(2,1)} %param.10) | copy-start | bytes 196612
  6.5 49.7 %copy-start.1 = (f32[16,128,128]{2,1,0:T(8,128)S(1)}, f32[16,128,128]{2,1,0:T(8,128)}, u32[]{:S(2)}) copy-start(f32[16,128,128]{2,1,0:T(8,128)} %param.11) | copy-start | bytes 3145732
  9.7 35.4 %all-to-all-start = ((s32[128,1,1]{2,1,0:T(1,128)}), s32[128,1,1]{2,1,0:T(1,128)S(1)}, u32[]{:S(2)}, u32[]{:S(2)}) async-start(s32[128,1,1]{2,1,0:T(1,128)} %copy.48), calls=%async_computation | async-start | bytes 131072 | tf_op jit(solution)/shard_map/all_to_all | solution.py:64
  49.6 61.0 %all-to-all-start.1 = ((bf16[32,128,1,128]{3,0,2,1:T(8,128)(2,1)}), bf16[32,128,1,128]{3,0,2,1:T(8,128)(2,1)S(1)}, u32[]{:S(2)}, u32[]{:S(2)}) async-start(bf16[32,128,1,128]{3,0,2,1:T(8,128)(2,1)} %copy.49), calls=%async_computation.1 | async-start | bytes 2097152 | tf_op jit(solution)/shard_map/all_to_all | solution.py:65
  56.2 58.0 %copy-start.3 = (s32[1,64]{1,0:T(1,128)S(1)}, s32[1,64]{1,0:T(1,128)}, u32[]{:S(2)}) copy-start(s32[1,64]{1,0:T(1,128)} %param.12) | copy-start | bytes 772
  56.2 55.1 %all-gather.2.cloned.1.call-start = ((), (), s32[]{:S(2)}) async-start(), calls=%async_computation.4 | async-start | bytes 2621440 | tf_op jit(solution)/shard_map/all_gather | solution.py:73
  116.7 62.8 %all-to-all-start.2 = ((bf16[32,128,1,128]{3,0,2,1:T(8,128)(2,1)}), bf16[32,128,1,128]{3,0,2,1:T(8,128)(2,1)S(1)}, u32[]{:S(2)}, u32[]{:S(2)}) async-start(bf16[32,128,1,128]{3,0,2,1:T(8,128)(2,1)} %copy.54), calls=%async_computation.2 | async-start | bytes 2097152 | tf_op jit(solution)/shard_map/all_to_all | solution.py:80
  125.2 91.1 %reduce-scatter.2.cloned.1.call-start = ((), (), s32[]{:S(2)}) async-start(), calls=%async_computation.5 | async-start | bytes 2621440 | tf_op jit(solution)/shard_map/reduce_scatter | solution.py:89
Sparse Core Ops, SparseCore 0:
  59.2 39.7 all-gather.1
  185.4 30.8 reduce-scatter.1
where the time goes:
time: 227 us; the launch traced here: 226 us
  waiting for transfers between devices  136 us (60%)
  starting transfers between devices  35.7 us (16%)
  local copies, waits for them, and re-layouts  18.4 us (8%)
  between operations  14.3 us (6%)
  matrix products  13.3 us (6%)
  other arithmetic  8.01 us (4%)
    all_to_all x1, waiting for transfers between devices, local(): lax.all_to_all(pick_tiles(data_tiles, wanted), 'var', split_axis=1, conca...  52.7 us
    all_to_all x1, waiting for transfers between devices, local(): lax.all_to_all(pick_tiles(image, wanted), 'var', split_axis=1, concat_axi...  45.7 us
    reduce_scatter x1, waiting for transfers between devices, local(): lax.psum_scatter(((first + second) * scale).astype(jnp.bfloat16), 'samp',...  23.8 us
    all_to_all x1, starting transfers between devices, local(): lax.all_to_all(own_table, 'var', split_axis=0, concat_axis=0, tiled=True)  20.4 us
    all_to_all x1, waiting for transfers between devices, local(): lax.all_to_all(own_table, 'var', split_axis=0, concat_axis=0, tiled=True)  14.1 us
    all_to_all x1, starting transfers between devices, local(): lax.all_to_all(pick_tiles(image, wanted), 'var', split_axis=1, concat_axi...  8.47 us
    all_to_all x1, starting transfers between devices, local(): lax.all_to_all(pick_tiles(data_tiles, wanted), 'var', split_axis=1, conca...  6.57 us
    unnamed x12, local copies, waits for them, and re-layouts  5.49 us
  transfers between devices with their start and end apart: 5, of which 4 were waited for; matrix products, arithmetic and copies ran while one was open for 8% of the time, Pallas kernels for 0%

commit v1 on v0

v1 whole, which is shorter than its diff:
```python
import jax
import jax.numpy as jnp
from jax import lax
from jax.experimental import pallas as pl
from jax.experimental.pallas import tpu as pltpu
from jax.sharding import PartitionSpec as P

penalty = 0.05

NX, NZ, NC, NY = 4, 16, 2, 4
GROUPS = NX * NC
HALF = NZ // 2
TILE = 128
TR = 8
KMAX = 64
NS = 32
SHARE = KMAX // NY
NSAMP = NS * NY
MESH = pl.DeviceIdType.MESH
BF = jnp.bfloat16


def kernel(
    data_ref, omega_ref, cols_ref, row_s, col_s, count_s, active_s, out_ref,
    *scratch,
):
    scratch = list(scratch)

    def take(n):
        got = scratch[:n]
        del scratch[:n]
        return got

    zbufs = [take(NZ), take(NZ)]
    stages = take(2)
    places = take(2)
    omega_all, lhs, picked, picked_image, rhs, rows, rows_t = take(7)
    want_v, want_s, slot_v, slot_s = take(4)
    zsend, zrecv, xsend, xrecv = take(4)
    wsend, wrecv, lsem = take(3)
    osend, orecv, ysend, yrecv = take(4)

    var = lax.axis_index("var")
    y = lax.axis_index("samp")
    x = var // (NZ * NC)
    z = lax.rem(var // NC, NZ)
    c = lax.rem(var, NC)

    def at(dx=0, dz=0, dc=0, dy=0):
        to = (lax.rem(x + dx, NX) * NZ + lax.rem(z + dz, NZ)) * NC + lax.rem(c + dc, NC)
        return (to, lax.rem(y + dy, NY))

    def remote(src, dst, send, recv, to):
        return pltpu.make_async_remote_copy(
            src_ref=src, dst_ref=dst, send_sem=send, recv_sem=recv, device_id=to, device_id_type=MESH
        )

    barrier = pltpu.get_barrier_semaphore()
    partners = [at(dz=1), at(dz=NZ - 1)]
    partners += [at(dx=g // NC, dc=g % NC) for g in range(1, GROUPS)]
    partners += [at(dy=d) for d in range(1, NY)]
    for to in partners:
        pl.semaphore_signal(barrier, inc=1, device_id=to, device_id_type=MESH)

    count = count_s[0]
    for t in range(TR):
        zbufs[0][0][t] = data_ref[:, t * TILE:(t + 1) * TILE]

    lane = lax.broadcasted_iota(jnp.int32, (1, TILE), 1)

    def want(k, held):
        col = col_s[0, k]
        owner = jnp.where(k < count, col // TR, -1)
        return jnp.where(lane == owner, lax.rem(col, TR), held)

    want_v[0] = lax.fori_loop(TR, KMAX, want, jnp.zeros((1, TILE), jnp.int32))

    cols = cols_ref[...]
    owner = cols // TR
    dx = lax.rem(owner // (NZ * NC) - x + NX, NX)
    dz = lax.rem(lax.rem(owner // NC, NZ) - z + NZ, NZ)
    dc = lax.rem(lax.rem(owner, NC) + c, NC)
    order = jnp.where(
        dz == 0, 0, jnp.where(dz < HALF, 2 * dz - 1, jnp.where(dz == HALF, NZ - 1, 2 * (NZ - dz)))
    )
    slot_v[...] = (dx * NC + dc) * NZ + order

    pl.semaphore_wait(barrier, len(partners))

    def zcopy(phase, side, step):
        bufs = zbufs[phase]
        src = bufs[0] if step == 1 else bufs[(step - 1) + side * HALF]
        dst = bufs[HALF] if step == HALF else bufs[step + side * HALF]
        if step == HALF:
            part = pl.ds(side * (TR // 2), TR // 2)
            src, dst = src.at[part], dst.at[part]
        index = side * HALF + step - 1
        return remote(
            src, dst, zsend.at[phase, index], zrecv.at[phase, index], at(dz=NZ - 1 if side else 1)
        )

    def select(phase, step):
        bufs, stage, place = zbufs[phase], stages[phase], places[phase]
        if step == 0:
            pieces, first = [(bufs[0], 0)], 0
        elif step < HALF:
            pieces, first = [(bufs[step + HALF], step), (bufs[step], NZ - step)], 2 * step - 1
        else:
            pieces, first = [(bufs[HALF], HALF)], NZ - 1

        def tile(g, buf, dz):
            wanted = want_s[g, 0, (x * NZ + lax.rem(z + dz, NZ)) * NC + c]
            return buf[wanted]

        def send(g, carry):
            for j, (buf, dz) in enumerate(pieces):
                stage[(g - 1) * NZ + first + j] = tile(g, buf, dz)
            dx, dc = g // NC, lax.rem(g, NC)
            there = lax.rem(NX - dx, NX) * NC + dc
            remote(
                stage.at[pl.ds((g - 1) * NZ + first, len(pieces))],
                place.at[pl.ds(there * NZ + first, len(pieces))],
                xsend.at[phase],
                xrecv.at[phase],
                at(dx=dx, dc=dc),
            ).start()
            return carry

        lax.fori_loop(1, GROUPS, send, 0)
        for j, (buf, dz) in enumerate(pieces):
            place[first + j] = tile(0, buf, dz)

    def gather(phase, hooks):
        for side in (0, 1):
            zcopy(phase, side, 1).start()
        if 0 in hooks:
            hooks[0]()
        select(phase, 0)
        for step in range(1, HALF + 1):
            for side in (0, 1):
                zcopy(phase, side, step).wait_recv()
                if step < HALF:
                    zcopy(phase, side, step + 1).start()
            select(phase, step)
            if step in hooks:
                hooks[step]()
        wait_all(phase).wait_recv()

    def wait_all(phase):
        count = (GROUPS - 1) * NZ
        return remote(
            stages[phase], places[phase].at[pl.ds(NZ, count)], xsend.at[phase], xrecv.at[phase], at(dx=1)
        )

    HALF_ROWS = SHARE * TILE // 2

    def ocopy(side, hop, half):
        owner = y if hop == 0 else lax.rem(y + (NY - 1 if side == 0 else 1), NY)
        part = omega_all.at[pl.ds(pl.multiple_of(owner * (2 * HALF_ROWS) + half * HALF_ROWS, HALF_ROWS), HALF_ROWS)]
        index = side * 3 + (2 if hop else half)
        return remote(part, part, osend.at[index], orecv.at[index], at(dy=1 if side == 0 else NY - 1))

    def wcopy(g):
        dx, dc = g // NC, g % NC
        there = ((NX - dx) % NX) * NC + dc
        return remote(want_v.at[0], want_v.at[there], wsend, wrecv, at(dx=dx, dc=dc))

    def start_hook():
        for g in range(1, GROUPS):
            wcopy(g).start()

        def cast(e, carry):
            low = omega_ref[e].astype(BF)
            omega_all[pl.ds(pl.multiple_of((y * SHARE + e) * TILE, TILE), TILE)] = low.T
            return carry

        lax.fori_loop(0, SHARE, cast, 0)
        for half in (0, 1):
            ocopy(0, 0, half).start()
            ocopy(1, 0, 1 - half).start()
        remote(want_v.at[pl.ds(1, GROUPS - 1)], want_v.at[pl.ds(1, GROUPS - 1)], wsend, wrecv, at(dx=1)).wait_recv()
        one = pltpu.make_async_copy(want_v, want_s, lsem.at[0])
        two = pltpu.make_async_copy(slot_v, slot_s, lsem.at[1])
        one.start()
        two.start()
        one.wait()
        two.wait()

    def forward_hook():
        ocopy(0, 0, 0).wait_recv()
        ocopy(0, 1, 0).start()
        ocopy(1, 0, 1).wait_recv()
        ocopy(1, 1, 1).start()

    gather(0, {0: start_hook, 4: forward_hook})

    own, place = zbufs[0][0], places[0]

    def put(k, tile):
        picked[k] = tile
        row = jnp.where(k < count, row_s[0, k], TR)
        for r in range(TR):
            lhs[r * NS:(r + 1) * NS, pl.ds(pl.multiple_of(k * TILE, TILE), TILE)] = jnp.where(
                row == r, tile, jnp.zeros_like(tile)
            )

    def put_own(k, carry):
        put(k, own[k])
        return carry

    def put_other(k, carry):
        put(k, place[slot_s[0, k]])
        return carry

    lax.fori_loop(0, TR, put_own, 0)
    lax.fori_loop(TR, KMAX, put_other, 0)

    def ycopy(kind, d):
        to = lax.rem(y + d, NY)
        here = pl.ds(pl.multiple_of(y * NS, NS), NS)
        there = pl.ds(pl.multiple_of(NSAMP + y * NS, NS), NS)
        mine = pl.ds(to * SHARE, SHARE)
        src, dst = (
            (picked.at[mine], rhs.at[:, here]),
            (zbufs[0][0], rows.at[:, there]),
            (zbufs[1][0], rows.at[:, here]),
            (picked_image.at[mine], rhs.at[:, there]),
        )[kind]
        return remote(src, dst, ysend.at[kind, d - 1], yrecv.at[kind, d - 1], at(dy=d))

    for side in (0, 1):
        ocopy(side, 0, 1 - side).wait_recv()
        ocopy(side, 1, side).wait_recv()

    CHUNK = 8 * TILE

    def multiply(i, total):
        part = pl.ds(pl.multiple_of(i * CHUNK, CHUNK), CHUNK)
        return total + jnp.dot(lhs[:, part], omega_all[part], preferred_element_type=jnp.float32)

    total = lax.fori_loop(0, KMAX * TILE // CHUNK, multiply, jnp.zeros((TR * NS, TILE), jnp.float32))
    image = total.astype(BF)
    for r in range(TR):
        zbufs[1][0][r] = image[r * NS:(r + 1) * NS]

    def y_hook():
        for kind in (0, 1, 2):
            for d in (1, 3, 2):
                ycopy(kind, d).start()

    gather(1, {0: y_hook})

    place = places[1]

    def image_own(k, carry):
        picked_image[k] = zbufs[1][0][k]
        return carry

    def image_other(k, carry):
        picked_image[k] = place[slot_s[0, k]]
        return carry

    lax.fori_loop(0, TR, image_own, 0)
    lax.fori_loop(TR, KMAX, image_other, 0)
    for d in (2, 1, 3):
        ycopy(3, d).start()

    here = pl.ds(pl.multiple_of(y * NS, NS), NS)
    there = pl.ds(pl.multiple_of(NSAMP + y * NS, NS), NS)
    for r in range(TR):
        rows[r, here] = zbufs[1][0][r]
        rows[r, there] = zbufs[0][0][r]

    def keep(e, carry):
        rhs[e, here] = picked[y * SHARE + e]
        rhs[e, there] = picked_image[y * SHARE + e]
        return carry

    lax.fori_loop(0, SHARE, keep, 0)
    for kind in (1, 2):
        for d in range(1, NY):
            ycopy(kind, d).wait_recv()
    for r in range(TR):
        rows_t[r] = rows[r].T
    for kind in (0, 3):
        for d in range(1, NY):
            ycopy(kind, d).wait_recv()

    eye = lax.broadcasted_iota(jnp.int32, (TILE, TILE), 0) == lax.broadcasted_iota(
        jnp.int32, (TILE, TILE), 1
    )

    def update(e, carry):
        k = y * SHARE + e
        gradient = jnp.dot(rows_t[row_s[0, k]], rhs[e], preferred_element_type=jnp.float32) * (0.5 / NSAMP)
        omega = omega_ref[e]
        on_diag = eye & (k < TR)
        gradient = gradient - jnp.where(on_diag, 1.0 / jnp.where(on_diag, omega, 1.0), 0.0)
        stepped = omega - gradient
        shrunk = stepped - jnp.minimum(jnp.maximum(stepped, -penalty), penalty)
        proximal = jnp.where(on_diag, stepped, shrunk)
        held = jnp.where(active_s[0, k] > 0, proximal, omega)
        out_ref[e] = jnp.where(k < count, held, 0.0)
        return carry

    lax.fori_loop(0, SHARE, update, 0)

    for phase in (0, 1):
        for side in (0, 1):
            for step in range(1, HALF + 1):
                zcopy(phase, side, step).wait_send()
        wait_all(phase).wait_send()
    remote(want_v.at[pl.ds(1, GROUPS - 1)], want_v.at[pl.ds(1, GROUPS - 1)], wsend, wrecv, at(dx=1)).wait_send()
    for side in (0, 1):
        for half in (0, 1):
            ocopy(side, 0, half).wait_send()
        ocopy(side, 1, side).wait_send()
    for kind in range(4):
        for d in range(1, NY):
            ycopy(kind, d).wait_send()


def local(data, omega, tile_row, tile_col, tile_count, tile_active):
    vmem = pl.BlockSpec(memory_space=pltpu.VMEM)
    smem = pl.BlockSpec(memory_space=pltpu.SMEM)
    block = pltpu.VMEM((TR, NS, TILE), BF)
    scratch = [block] * (2 * NZ)
    scratch += [pltpu.VMEM(((GROUPS - 1) * NZ, NS, TILE), BF)] * 2
    scratch += [pltpu.VMEM((GROUPS * NZ, NS, TILE), BF)] * 2
    scratch += [
        pltpu.VMEM((KMAX * TILE, TILE), BF),
        pltpu.VMEM((TR * NS, KMAX * TILE), BF),
        pltpu.VMEM((KMAX, NS, TILE), BF),
        pltpu.VMEM((KMAX, NS, TILE), BF),
        pltpu.VMEM((SHARE, 2 * NSAMP, TILE), BF),
        pltpu.VMEM((TR, 2 * NSAMP, TILE), BF),
        pltpu.VMEM((TR, TILE, 2 * NSAMP), BF),
        pltpu.VMEM((GROUPS, 1, TILE), jnp.int32),
        pltpu.SMEM((GROUPS, 1, TILE), jnp.int32),
        pltpu.VMEM((1, KMAX), jnp.int32),
        pltpu.SMEM((1, KMAX), jnp.int32),
    ]
    dma = pltpu.SemaphoreType.DMA
    scratch += [dma((2, NZ)), dma((2, NZ)), dma((2,)), dma((2,))]
    scratch += [dma, dma, dma((2,))]
    scratch += [dma((6,)), dma((6,)), dma((4, NY - 1)), dma((4, NY - 1))]
    return pl.pallas_call(
        kernel,
        out_shape=jax.ShapeDtypeStruct(omega.shape, omega.dtype),
        in_specs=[vmem, vmem, vmem, smem, smem, smem, smem],
        out_specs=vmem,
        scratch_shapes=scratch,
        compiler_params=pltpu.CompilerParams(
            collective_id=0, has_side_effects=True, vmem_limit_bytes=40 * 2**20
        ),
    )(data, omega, tile_col, tile_row, tile_col, tile_count, tile_active)


def solution(mesh):
    placed = (
        P("samp", "var"),
        P(("var", "samp"), None, None),
        P("var", None),
        P("var", None),
        P("var"),
        P("var", None),
    )
    return jax.shard_map(
        local, mesh=mesh, in_specs=placed, out_specs=P(("var", "samp"), None, None), check_vma=False
    )
```

time: 227 us -> 99.7 us (0.44)
  waiting for transfers between devices: 136 us -> 0 us
  Pallas kernels: 0 us -> 95.7 us
  starting transfers between devices: 35.7 us -> 0 us
  local copies, waits for them, and re-layouts: 18.4 us -> 3.04 us
  between operations: 14.3 us -> 0.74 us
  matrix products: 13.3 us -> 0 us
  other arithmetic: 8.01 us -> 0 us
    all_to_all x3 -> x0, waiting for transfers between devices: 113 us -> none  [the longest x1 52.7 us: local(): lax.all_to_all(pick_tiles(data_tiles, wanted), 'var', split_axis=1, conca...]
    pallas_call x0 -> x1, Pallas kernels: none -> 95.7 us  [local(): pl.pallas_call(kernel, out_shape=jax.ShapeDtypeStruct(omega.shape, omega....]
    all_to_all x3 -> x0, starting transfers between devices: 35.4 us -> none  [the longest x1 20.4 us: local(): lax.all_to_all(own_table, 'var', split_axis=0, concat_axis=0, tiled=True)]
    reduce_scatter x1 -> x0, waiting for transfers between devices: 23.8 us -> none  [local(): lax.psum_scatter(((first + second) * scale).astype(jnp.bfloat16), 'samp',...]
    dot_general x6 -> x0, matrix products: 13.3 us -> none  [the longest x1 5.04 us: local(): jnp.einsum('sku,skt->kut', row_data, col_image, preferred_element_type=jn...]
    gather x8 -> x0, local copies, waits for them, and re-layouts: 8.72 us -> none  [the longest x2 2.08 us: place_tiles(): own_part = jnp.take(own_tiles, local_index, axis=1)]
    select_n x6 -> x0, other arithmetic: 3.67 us -> none  [the longest x1 2.89 us: local(): return jnp.where(share_live[:, None, None], held, 0.0)]
    convert_element_type x3 -> x0, local copies, waits for them, and re-layouts: 3.34 us -> none  [the longest x2 3.32 us: pick_tiles(): return picked.astype(jnp.bfloat16)]
  transfers between devices with their start and end apart: 5 -> 0, of which waited for: 4 -> 0; matrix products, arithmetic and copies ran while one was open for 8% -> 0% of each run, Pallas kernels for 0% -> 0%
where the time goes in v1:
time: 99.7 us; the launch traced here: 99.5 us
  Pallas kernels  95.7 us (96%)
  local copies, waits for them, and re-layouts  3.04 us (3%)
    pallas_call x1, Pallas kernels, local(): pl.pallas_call(kernel, out_shape=jax.ShapeDtypeStruct(omega.shape, omega....  95.7 us
    unnamed x11, local copies, waits for them, and re-layouts  3.04 us

profile of v1, /device:TPU:1, one launch (start us, length us, event | category | flops | bytes accessed | tf_op | source)
XLA Modules:
  0.0 99.5 jit_solution(4867414768452431869)
XLA Ops:
  0.0 0.0 copy-start.4
  0.0 0.0 copy-start.2
  0.0 0.0 copy-start.3
  0.7 0.0 copy-done.4
  0.7 0.0 copy-done.2
  0.7 0.0 copy-done.3
  0.7 0.0 copy-start
  0.7 1.2 %copy-done = f32[16,128,128]{2,1,0:T(8,128)S(1)} copy-done((f32[16,128,128]{2,1,0:T(8,128)S(1)}, f32[16,128,128]{2,1,0:T(8,128)}, u32[]{:S(2)}) %copy-start) | copy-done | bytes 1048600
  2.0 0.0 copy-start.1
  2.0 0.8 copy-done.1
  2.8 95.7 %shard_map.64 = f32[16,128,128]{2,1,0:T(8,128)S(1)} custom-call(bf16[32,1024]{1,0:T(8,128)(2,1)S(1)} %copy-done.1, f32[16,128,128]{2,1,0:T(8,128)S(1)} %copy-done, s32[1,64]{1,0:T(1,128)S(1)} %copy-done.2, s32[1,64]{1,0:T(1,128)S(1)} %copy-done.3, s32[1,64]{1,0:T(1,128)S(1)} %copy-done.2, s32[1]{0:T(128)S(6)} %copy.8.count_s, s32[1,64]{1,0:T(1,128)S(1)} %copy-done.4), custom_call_target="tpu_custom_call" | custom-call | tf_op jit(solution)/shard_map/pallas_call | solution.py:347
  98.5 1.0 copy.9
Async XLA Ops:
  0.0 0.7 copy-start.4
  0.0 0.7 copy-start.2
  0.0 0.7 copy-start.3
  0.7 1.2 %copy-start = (f32[16,128,128]{2,1,0:T(8,128)S(1)}, f32[16,128,128]{2,1,0:T(8,128)}, u32[]{:S(2)}) copy-start(f32[16,128,128]{2,1,0:T(8,128)} %omega_ref.1) | copy-start | bytes 3145732
  2.0 0.8 copy-start.1

commit v2 on v1

--- a/solution.py
+++ b/solution.py
@@ -8,8 +8,12 @@
 penalty = 0.05
 
 NX, NZ, NC, NY = 4, 16, 2, 4
-GROUPS = NX * NC
-HALF = NZ // 2
+STRIDE = 3
+CHUNKS = 5
+PLANE = NX * NC
+GROUPS = PLANE * STRIDE
+LOCAL = 1 + CHUNKS
+SLOTS = GROUPS * CHUNKS + PLANE
 TILE = 128
 TR = 8
 KMAX = 64
@@ -20,8 +24,18 @@
 BF = jnp.bfloat16
 
 
+def split(g):
+    i = g % STRIDE
+    return g // (NC * STRIDE), (0, 1, NZ - 1)[i], (g // STRIDE) % NC
+
+
+def mirrored(g):
+    dx, dc, i = g // (NC * STRIDE), (g // STRIDE) % NC, g % STRIDE
+    return (((NX - dx) % NX) * NC + dc) * STRIDE + (STRIDE - i) % STRIDE
+
+
 def kernel(
-    data_ref, omega_ref, cols_ref, row_s, col_s, count_s, active_s, out_ref,
+    data_hbm, omega_hbm, cols_ref, row_s, col_s, count_s, active_s, out_ref,
     *scratch,
 ):
     scratch = list(scratch)
@@ -31,24 +45,38 @@
         del scratch[:n]
         return got
 
-    zbufs = [take(NZ), take(NZ)]
+    zbufs = [take(CHUNKS + 1), take(CHUNKS + 1)]
     stages = take(2)
     places = take(2)
+    data_ref, omega_ref = take(2)
     omega_all, lhs, picked, picked_image, rhs, rows, rows_t = take(7)
     want_v, want_s, slot_v, slot_s = take(4)
     zsend, zrecv, xsend, xrecv = take(4)
     wsend, wrecv, lsem = take(3)
     osend, orecv, ysend, yrecv = take(4)
 
+    load_data = pltpu.make_async_copy(data_hbm, data_ref, lsem.at[2])
+    load_omega = pltpu.make_async_copy(omega_hbm, omega_ref, lsem.at[3])
+    load_data.start()
+    load_omega.start()
+
     var = lax.axis_index("var")
     y = lax.axis_index("samp")
     x = var // (NZ * NC)
     z = lax.rem(var // NC, NZ)
     c = lax.rem(var, NC)
 
+    xs = [x] + [lax.rem(x + d, NX) for d in range(1, NX)]
+    zs = [z] + [lax.rem(z + d, NZ) for d in range(1, NZ)]
+    cs = [c, 1 - c]
+    ys = [y] + [lax.rem(y + d, NY) for d in range(1, NY)]
+
     def at(dx=0, dz=0, dc=0, dy=0):
-        to = (lax.rem(x + dx, NX) * NZ + lax.rem(z + dz, NZ)) * NC + lax.rem(c + dc, NC)
-        return (to, lax.rem(y + dy, NY))
+        return ((xs[dx] * NZ + zs[dz % NZ]) * NC + cs[dc], ys[dy])
+
+    def served(g):
+        dx, dz, dc = split(g)
+        return at(dx=dx, dz=dz, dc=dc)
 
     def remote(src, dst, send, recv, to):
         return pltpu.make_async_remote_copy(
@@ -56,15 +84,13 @@
         )
 
     barrier = pltpu.get_barrier_semaphore()
-    partners = [at(dz=1), at(dz=NZ - 1)]
-    partners += [at(dx=g // NC, dc=g % NC) for g in range(1, GROUPS)]
+    partners = [served(g) for g in range(1, GROUPS)]
+    partners += [at(dz=dz) for dz in (STRIDE, NZ - STRIDE, 2, NZ - 2)]
     partners += [at(dy=d) for d in range(1, NY)]
     for to in partners:
         pl.semaphore_signal(barrier, inc=1, device_id=to, device_id_type=MESH)
 
     count = count_s[0]
-    for t in range(TR):
-        zbufs[0][0][t] = data_ref[:, t * TILE:(t + 1) * TILE]
 
     lane = lax.broadcasted_iota(jnp.int32, (1, TILE), 1)
 
@@ -80,76 +106,91 @@
     dx = lax.rem(owner // (NZ * NC) - x + NX, NX)
     dz = lax.rem(lax.rem(owner // NC, NZ) - z + NZ, NZ)
     dc = lax.rem(lax.rem(owner, NC) + c, NC)
-    order = jnp.where(
-        dz == 0, 0, jnp.where(dz < HALF, 2 * dz - 1, jnp.where(dz == HALF, NZ - 1, 2 * (NZ - dz)))
+    opposite = dz == NZ // 2
+    step = lax.rem(dz + NZ // 2 - 1, NZ)
+    side = lax.rem(step, STRIDE)
+    far = step // STRIDE
+    side = jnp.where(side == 0, 2, side - 1)
+    far = jnp.where(far == 2, 0, jnp.where(far == 3, 1, jnp.where(far == 1, 2, jnp.where(far == 4, 3, 4))))
+    plane = dx * NC + dc
+    slot_v[...] = jnp.where(
+        opposite,
+        jnp.where(plane == 0, 0, SLOTS - PLANE + plane),
+        1 + (plane * STRIDE + side) * CHUNKS + far,
     )
-    slot_v[...] = (dx * NC + dc) * NZ + order
+
+    load_data.wait()
+    for t in range(TR):
+        zbufs[0][0][t] = data_ref[:, t * TILE:(t + 1) * TILE]
 
     pl.semaphore_wait(barrier, len(partners))
 
-    def zcopy(phase, side, step):
+    PLACES = (0, STRIDE, NZ - STRIDE, 2 * STRIDE, NZ - 2 * STRIDE, NZ // 2)
+
+    def zcopy(phase, j):
         bufs = zbufs[phase]
-        src = bufs[0] if step == 1 else bufs[(step - 1) + side * HALF]
-        dst = bufs[HALF] if step == HALF else bufs[step + side * HALF]
-        if step == HALF:
-            part = pl.ds(side * (TR // 2), TR // 2)
+        src, dst = bufs[max(j - 2, 0)], bufs[min(j, CHUNKS)]
+        dz = STRIDE if j <= 4 else 2
+        if j > 4:
+            part = pl.ds((j - 5) * (TR // 2), TR // 2)
             src, dst = src.at[part], dst.at[part]
-        index = side * HALF + step - 1
         return remote(
-            src, dst, zsend.at[phase, index], zrecv.at[phase, index], at(dz=NZ - 1 if side else 1)
+            src, dst, zsend.at[phase, j - 1], zrecv.at[phase, j - 1], at(dz=NZ - dz if j % 2 else dz)
         )
 
-    def select(phase, step):
+    def select(phase, first, number):
         bufs, stage, place = zbufs[phase], stages[phase], places[phase]
-        if step == 0:
-            pieces, first = [(bufs[0], 0)], 0
-        elif step < HALF:
-            pieces, first = [(bufs[step + HALF], step), (bufs[step], NZ - step)], 2 * step - 1
-        else:
-            pieces, first = [(bufs[HALF], HALF)], NZ - 1
-
-        def tile(g, buf, dz):
-            wanted = want_s[g, 0, (x * NZ + lax.rem(z + dz, NZ)) * NC + c]
-            return buf[wanted]
-
-        def send(g, carry):
-            for j, (buf, dz) in enumerate(pieces):
-                stage[(g - 1) * NZ + first + j] = tile(g, buf, dz)
-            dx, dc = g // NC, lax.rem(g, NC)
-            there = lax.rem(NX - dx, NX) * NC + dc
+        pieces = range(first, first + number)
+        last = first == CHUNKS
+
+        def tile(g, j):
+            return bufs[j][want_s[g, 0, at(dz=PLACES[j])[0]]]
+
+        for g in range(STRIDE if last else 1, GROUPS, STRIDE if last else 1):
+            if last:
+                here = GROUPS * CHUNKS - LOCAL + g // STRIDE
+                there = GROUPS * CHUNKS + mirrored(g) // STRIDE
+            else:
+                here = 1 + g * CHUNKS + first - LOCAL
+                there = 1 + mirrored(g) * CHUNKS + first
+            for j in pieces:
+                stage[here + j - first] = tile(g, j)
             remote(
-                stage.at[pl.ds((g - 1) * NZ + first, len(pieces))],
-                place.at[pl.ds(there * NZ + first, len(pieces))],
+                stage.at[pl.ds(here, number)],
+                place.at[pl.ds(there, number)],
                 xsend.at[phase],
                 xrecv.at[phase],
-                at(dx=dx, dc=dc),
+                served(g),
             ).start()
-            return carry
-
-        lax.fori_loop(1, GROUPS, send, 0)
-        for j, (buf, dz) in enumerate(pieces):
-            place[first + j] = tile(0, buf, dz)
+        for j in pieces:
+            place[0 if last else 1 + j] = tile(0, j)
 
     def gather(phase, hooks):
-        for side in (0, 1):
-            zcopy(phase, side, 1).start()
-        if 0 in hooks:
-            hooks[0]()
-        select(phase, 0)
-        for step in range(1, HALF + 1):
-            for side in (0, 1):
-                zcopy(phase, side, step).wait_recv()
-                if step < HALF:
-                    zcopy(phase, side, step + 1).start()
-            select(phase, step)
-            if step in hooks:
-                hooks[step]()
+        zcopy(phase, 1).start()
+        zcopy(phase, 2).start()
+        hooks[0]()
+        if phase:
+            select(phase, 0, 1)
+        for j in (1, 2):
+            zcopy(phase, j).wait_recv()
+            zcopy(phase, j + 2).start()
+        hooks[1]()
+        if not phase:
+            select(phase, 0, 1)
+        select(phase, 1, 2)
+        for j in (3, 4):
+            zcopy(phase, j).wait_recv()
+            zcopy(phase, j + 2).start()
+        hooks[2]()
+        select(phase, 3, 2)
+        zcopy(phase, 5).wait_recv()
+        zcopy(phase, 6).wait_recv()
+        select(phase, CHUNKS, 1)
         wait_all(phase).wait_recv()
 
     def wait_all(phase):
-        count = (GROUPS - 1) * NZ
         return remote(
-            stages[phase], places[phase].at[pl.ds(NZ, count)], xsend.at[phase], xrecv.at[phase], at(dx=1)
+            stages[phase], places[phase].at[pl.ds(LOCAL, SLOTS - LOCAL)], xsend.at[phase], xrecv.at[phase], at(dx=1)
         )
 
     HALF_ROWS = SHARE * TILE // 2
@@ -160,14 +201,11 @@
         index = side * 3 + (2 if hop else half)
         return remote(part, part, osend.at[index], orecv.at[index], at(dy=1 if side == 0 else NY - 1))
 
-    def wcopy(g):
-        dx, dc = g // NC, g % NC
-        there = ((NX - dx) % NX) * NC + dc
-        return remote(want_v.at[0], want_v.at[there], wsend, wrecv, at(dx=dx, dc=dc))
 
     def start_hook():
         for g in range(1, GROUPS):
-            wcopy(g).start()
+            remote(want_v.at[0], want_v.at[mirrored(g)], wsend, wrecv, served(g)).start()
+        load_omega.wait()
 
         def cast(e, carry):
             low = omega_ref[e].astype(BF)
@@ -178,6 +216,8 @@
         for half in (0, 1):
             ocopy(0, 0, half).start()
             ocopy(1, 0, 1 - half).start()
+
+    def table_hook():
         remote(want_v.at[pl.ds(1, GROUPS - 1)], want_v.at[pl.ds(1, GROUPS - 1)], wsend, wrecv, at(dx=1)).wait_recv()
         one = pltpu.make_async_copy(want_v, want_s, lsem.at[0])
         two = pltpu.make_async_copy(slot_v, slot_s, lsem.at[1])
@@ -192,7 +232,7 @@
         ocopy(1, 0, 1).wait_recv()
         ocopy(1, 1, 1).start()
 
-    gather(0, {0: start_hook, 4: forward_hook})
+    gather(0, (start_hook, table_hook, forward_hook))
 
     own, place = zbufs[0][0], places[0]
 
@@ -248,7 +288,7 @@
             for d in (1, 3, 2):
                 ycopy(kind, d).start()
 
-    gather(1, {0: y_hook})
+    gather(1, (y_hook, lambda: None, lambda: None))
 
     place = places[1]
 
@@ -306,9 +346,8 @@
     lax.fori_loop(0, SHARE, update, 0)
 
     for phase in (0, 1):
-        for side in (0, 1):
-            for step in range(1, HALF + 1):
-                zcopy(phase, side, step).wait_send()
+        for j in range(1, 7):
+            zcopy(phase, j).wait_send()
         wait_all(phase).wait_send()
     remote(want_v.at[pl.ds(1, GROUPS - 1)], want_v.at[pl.ds(1, GROUPS - 1)], wsend, wrecv, at(dx=1)).wait_send()
     for side in (0, 1):
@@ -322,11 +361,13 @@
 
 def local(data, omega, tile_row, tile_col, tile_count, tile_active):
     vmem = pl.BlockSpec(memory_space=pltpu.VMEM)
+    hbm = pl.BlockSpec(memory_space=pltpu.HBM)
     smem = pl.BlockSpec(memory_space=pltpu.SMEM)
     block = pltpu.VMEM((TR, NS, TILE), BF)
-    scratch = [block] * (2 * NZ)
-    scratch += [pltpu.VMEM(((GROUPS - 1) * NZ, NS, TILE), BF)] * 2
-    scratch += [pltpu.VMEM((GROUPS * NZ, NS, TILE), BF)] * 2
+    scratch = [block] * (2 * (CHUNKS + 1))
+    scratch += [pltpu.VMEM((SLOTS - LOCAL, NS, TILE), BF)] * 2
+    scratch += [pltpu.VMEM((SLOTS, NS, TILE), BF)] * 2
+    scratch += [pltpu.VMEM(data.shape, data.dtype), pltpu.VMEM(omega.shape, omega.dtype)]
     scratch += [
         pltpu.VMEM((KMAX * TILE, TILE), BF),
         pltpu.VMEM((TR * NS, KMAX * TILE), BF),
@@ -341,17 +382,17 @@
         pltpu.SMEM((1, KMAX), jnp.int32),
     ]
     dma = pltpu.SemaphoreType.DMA
-    scratch += [dma((2, NZ)), dma((2, NZ)), dma((2,)), dma((2,))]
-    scratch += [dma, dma, dma((2,))]
+    scratch += [dma((2, 6)), dma((2, 6)), dma((2,)), dma((2,))]
+    scratch += [dma, dma, dma((4,))]
     scratch += [dma((6,)), dma((6,)), dma((4, NY - 1)), dma((4, NY - 1))]
     return pl.pallas_call(
         kernel,
         out_shape=jax.ShapeDtypeStruct(omega.shape, omega.dtype),
-        in_specs=[vmem, vmem, vmem, smem, smem, smem, smem],
+        in_specs=[hbm, hbm, vmem, smem, smem, smem, smem],
         out_specs=vmem,
         scratch_shapes=scratch,
         compiler_params=pltpu.CompilerParams(
-            collective_id=0, has_side_effects=True, vmem_limit_bytes=40 * 2**20
+            collective_id=0, has_side_effects=True, vmem_limit_bytes=60 * 2**20
         ),
     )(data, omega, tile_col, tile_row, tile_col, tile_count, tile_active)
 

time: 99.7 us -> 82.5 us (0.83)
  Pallas kernels: 95.7 us -> 79.4 us
    pallas_call x1, Pallas kernels: 95.7 us -> 79.4 us  [local(): pl.pallas_call(kernel, out_shape=jax.ShapeDtypeStruct(omega.shape, omega....]
    unnamed x11 -> x1, local copies, waits for them, and re-layouts: 3.04 us -> 2.3 us
where the time goes in v2:
time: 82.5 us; the launch traced here: 82.3 us
  Pallas kernels  79.4 us (96%)
  local copies, waits for them, and re-layouts  2.3 us (3%)
    pallas_call x1, Pallas kernels, local(): pl.pallas_call(kernel, out_shape=jax.ShapeDtypeStruct(omega.shape, omega....  79.4 us
    unnamed x1, local copies, waits for them, and re-layouts  2.3 us

profile of v2, /device:TPU:1, one launch (start us, length us, event | category | flops | bytes accessed | tf_op | source)
XLA Modules:
  0.0 82.3 jit_solution(11716011135696020704)
XLA Ops:
  0.7 79.4 %shard_map.64 = f32[16,128,128]{2,1,0:T(8,128)} custom-call(bf16[32,1024]{1,0:T(8,128)(2,1)} %data_hbm.1, f32[16,128,128]{2,1,0:T(8,128)} %omega_hbm.1, s32[1,64]{1,0:T(1,128)} %col_s.1, s32[1,64]{1,0:T(1,128)} %row_s.1, s32[1,64]{1,0:T(1,128)} %col_s.1, s32[1]{0:T(128)S(6)} %copy.8.count_s, s32[1,64]{1,0:T(1,128)} %active_s.1), custom_call_target="tpu_custom_call" | custom-call | tf_op jit(solution)/shard_map/pallas_call | solution.py:388
  80.0 2.3 %copy.9 = f32[16,128,128]{2,1,0:T(8,128)} copy(f32[16,128,128]{2,1,0:T(8,128)} %shard_map.64) | data formatting | bytes 2097152

commit v3 on v2

v3 whole, which is shorter than its diff:
```python
import jax
import jax.numpy as jnp
from jax import lax
from jax.experimental import pallas as pl
from jax.experimental.pallas import tpu as pltpu
from jax.sharding import PartitionSpec as P

penalty = 0.05

NX, NZ, NC, NY = 4, 16, 2, 4
STRIDE = 3
CHUNKS = 5
PLANE = NX * NC
GROUPS = PLANE * STRIDE
LOCAL = CHUNKS
SLOTS = GROUPS * CHUNKS + PLANE
TILE = 128
TR = 8
KMAX = 64
NS = 32
SHARE = KMAX // NY
NSAMP = NS * NY
MESH = pl.DeviceIdType.MESH
BF = jnp.bfloat16


def split(g):
    if g >= GROUPS:
        dx, dc = (g - GROUPS) // NC, g % NC
        return dx, NZ - 2 if dc else 2, dc
    return g // (NC * STRIDE), (0, 1, NZ - 1)[g % STRIDE], (g // STRIDE) % NC


def mirrored(g):
    if g >= GROUPS:
        dx, dc = (g - GROUPS) // NC, g % NC
        return GROUPS + ((NX - dx) % NX) * NC + dc
    dx, dc, i = g // (NC * STRIDE), (g // STRIDE) % NC, g % STRIDE
    return (((NX - dx) % NX) * NC + dc) * STRIDE + (STRIDE - i) % STRIDE


AROUND = (0, 1, NZ - 1, 2, NZ - 2)


def kernel(
    data_hbm, omega_hbm, cols_ref, row_s, col_s, count_s, active_s, out_ref,
    *scratch,
):
    scratch = list(scratch)

    def take(n):
        got = scratch[:n]
        del scratch[:n]
        return got

    zbufs = [take(CHUNKS), take(CHUNKS)]
    stages = take(2)
    places = take(2)
    data_ref, omega_ref = take(2)
    omega_all, lhs, picked, picked_image, rhs, rhs_image, started, rows, rows_t = take(9)
    want_v, want_s, slot_v, slot_s = take(4)
    zsend, zrecv, xsend, xrecv = take(4)
    wsend, wrecv, lsem = take(3)
    osend, orecv, ysend, yrecv = take(4)

    load_data = pltpu.make_async_copy(data_hbm, data_ref, lsem.at[2])
    load_omega = pltpu.make_async_copy(omega_hbm, omega_ref, lsem.at[3])
    load_data.start()
    load_omega.start()

    var = lax.axis_index("var")
    y = lax.axis_index("samp")
    x = var // (NZ * NC)
    z = lax.rem(var // NC, NZ)
    c = lax.rem(var, NC)

    xs = [x] + [lax.rem(x + d, NX) for d in range(1, NX)]
    zs = [z] + [lax.rem(z + d, NZ) for d in range(1, NZ)]
    cs = [c, 1 - c]
    ys = [y] + [lax.rem(y + d, NY) for d in range(1, NY)]

    def at(dx=0, dz=0, dc=0, dy=0):
        return ((xs[dx] * NZ + zs[dz % NZ]) * NC + cs[dc], ys[dy])

    def served(g):
        dx, dz, dc = split(g)
        return at(dx=dx, dz=dz, dc=dc)

    def remote(src, dst, send, recv, to):
        return pltpu.make_async_remote_copy(
            src_ref=src, dst_ref=dst, send_sem=send, recv_sem=recv, device_id=to, device_id_type=MESH
        )

    barrier = pltpu.get_barrier_semaphore()
    partners = [at(dx=p // NC, dc=p % NC) for p in range(1, PLANE)]
    partners += [at(dz=dz) for dz in (1, 2, 3, NZ - 3, NZ - 2, NZ - 1)]
    partners += [at(dy=d) for d in range(1, NY)]
    for to in partners:
        pl.semaphore_signal(barrier, inc=1, device_id=to, device_id_type=MESH)

    count = count_s[0]

    lane = lax.broadcasted_iota(jnp.int32, (1, TILE), 1)

    def want(k, held):
        col = col_s[0, k]
        owner = jnp.where(k < count, col // TR, -1)
        return jnp.where(lane == owner, lax.rem(col, TR), held)

    want_v[0] = lax.fori_loop(TR, KMAX, want, jnp.zeros((1, TILE), jnp.int32), unroll=8)

    cols = cols_ref[...]
    owner = cols // TR
    dx = lax.rem(owner // (NZ * NC) - x + NX, NX)
    dz = lax.rem(lax.rem(owner // NC, NZ) - z + NZ, NZ)
    dc = lax.rem(lax.rem(owner, NC) + c, NC)
    opposite = dz == NZ // 2
    step = lax.rem(dz + NZ // 2 - 1, NZ)
    side = lax.rem(step, STRIDE)
    far = step // STRIDE
    side = jnp.where(side == 0, 2, side - 1)
    far = jnp.where(far == 2, 0, jnp.where(far == 3, 1, jnp.where(far == 1, 2, jnp.where(far == 4, 3, 4))))
    plane = dx * NC + dc
    slot_v[...] = jnp.where(
        opposite,
        GROUPS * CHUNKS + plane,
        (plane * STRIDE + side) * CHUNKS + far,
    )

    load_data.wait()
    for t in range(TR):
        zbufs[0][0][t] = data_ref[:, t * TILE:(t + 1) * TILE]

    pl.semaphore_wait(barrier, len(partners))

    PLACES = (0, STRIDE, NZ - STRIDE, 2 * STRIDE, NZ - 2 * STRIDE)

    def zcopy(phase, j):
        bufs = zbufs[phase]
        return remote(
            bufs[max(j - 2, 0)],
            bufs[j],
            zsend.at[phase, j - 1],
            zrecv.at[phase, j - 1],
            at(dz=NZ - STRIDE if j % 2 else STRIDE),
        )

    def select(phase, first, number):
        bufs, stage, place = zbufs[phase], stages[phase], places[phase]

        def tile(g, j):
            dx, dz, dc = split(g)
            table = AROUND.index(dz) * PLANE + dx * NC + dc
            return bufs[j][want_s[table, 0, at(dz=PLACES[j])[0]]]

        def send(g, here, there, pieces):
            for n, j in enumerate(pieces):
                stage[here + n] = tile(g, j)
            remote(
                stage.at[pl.ds(here, len(pieces))],
                place.at[pl.ds(there, len(pieces))],
                xsend.at[phase],
                xrecv.at[phase],
                served(g),
            ).start()

        pieces = range(first, first + number)
        if first == 3:
            for g in range(GROUPS, GROUPS + PLANE):
                base = GROUPS * CHUNKS - GROUPS
                send(g, base + g - LOCAL, base + mirrored(g), (3,) if g % NC else (4,))
        for g in range(1, GROUPS):
            send(g, g * CHUNKS + first - LOCAL, mirrored(g) * CHUNKS + first, pieces)
        for j in pieces:
            place[j] = tile(0, j)

    def gather(phase, hooks):
        zcopy(phase, 1).start()
        zcopy(phase, 2).start()
        hooks[0]()
        if phase and True:
            select(phase, 0, 1)
        for j in (1, 2):
            zcopy(phase, j).wait_recv()
            zcopy(phase, j + 2).start()
        hooks[1]()
        if not (phase and True):
            select(phase, 0, 1)
        select(phase, 1, 2)
        hooks[2]()
        for j in (3, 4):
            zcopy(phase, j).wait_recv()
        select(phase, 3, 2)
        hooks[3]()
        wait_all(phase).wait_recv()

    def wait_all(phase):
        return remote(
            stages[phase], places[phase].at[pl.ds(LOCAL, SLOTS - LOCAL)], xsend.at[phase], xrecv.at[phase], at(dx=1)
        )

    HALF_ROWS = SHARE * TILE // 2

    def ocopy(side, hop, half):
        owner = y if hop == 0 else lax.rem(y + (NY - 1 if side == 0 else 1), NY)
        part = omega_all.at[pl.ds(pl.multiple_of(owner * (2 * HALF_ROWS) + half * HALF_ROWS, HALF_ROWS), HALF_ROWS)]
        index = side * 3 + (2 if hop else half)
        return remote(part, part, osend.at[index], orecv.at[index], at(dy=1 if side == 0 else NY - 1))


    def wcopy(p):
        dx, dc = p // NC, p % NC
        there = ((NX - dx) % NX) * NC + dc
        return remote(want_v.at[0], want_v.at[there], wsend.at[0], wrecv.at[0], at(dx=dx, dc=dc))

    def wplane():
        part = want_v.at[pl.ds(1, PLANE - 1)]
        return remote(part, part, wsend.at[0], wrecv.at[0], at(dx=1))

    def wforward(i):
        there = want_v.at[pl.ds(i * PLANE, PLANE)]
        return remote(want_v.at[pl.ds(0, PLANE)], there, wsend.at[i], wrecv.at[i], at(dz=NZ - AROUND[i]))

    def start_hook():
        for p in range(1, PLANE):
            wcopy(p).start()
        load_omega.wait()

        wplane().wait_recv()
        for i in range(1, len(AROUND)):
            wforward(i).start()

        def cast(e, carry):
            low = omega_ref[e].astype(BF)
            omega_all[pl.ds(pl.multiple_of((y * SHARE + e) * TILE, TILE), TILE)] = low.T
            return carry

        lax.fori_loop(0, SHARE, cast, 0, unroll=4)
        for half in (0, 1):
            ocopy(0, 0, half).start()
            ocopy(1, 0, 1 - half).start()

    def table_hook():
        for i in range(1, len(AROUND)):
            wforward(i).wait_recv()
        one = pltpu.make_async_copy(want_v, want_s, lsem.at[0])
        two = pltpu.make_async_copy(slot_v, slot_s, lsem.at[1])
        one.start()
        two.start()
        one.wait()
        two.wait()

    def forward_hook():
        ocopy(0, 0, 0).wait_recv()
        ocopy(0, 1, 0).start()
        ocopy(1, 0, 1).wait_recv()
        ocopy(1, 1, 1).start()

    gather(0, (start_hook, table_hook, forward_hook, lambda: None))

    own, place = zbufs[0][0], places[0]

    def put(k, tile):
        picked[k] = tile
        row = jnp.where(k < count, row_s[0, k], TR)
        for r in range(TR):
            lhs[r * NS:(r + 1) * NS, pl.ds(pl.multiple_of(k * TILE, TILE), TILE)] = jnp.where(
                row == r, tile, jnp.zeros_like(tile)
            )

    def put_own(k, carry):
        put(k, own[k])
        return carry

    def put_other(k, carry):
        put(k, place[slot_s[0, k]])
        return carry

    lax.fori_loop(0, TR, put_own, 0, unroll=4)
    lax.fori_loop(TR, KMAX, put_other, 0, unroll=4)

    def ycopy(kind, d):
        to = lax.rem(y + d, NY)
        here = pl.ds(pl.multiple_of(y * NS, NS), NS)
        there = pl.ds(pl.multiple_of(NSAMP + y * NS, NS), NS)
        mine = pl.ds(to * SHARE, SHARE)
        src, dst = (
            (picked.at[mine], rhs.at[:, here]),
            (zbufs[0][0], rows.at[:, there]),
            (zbufs[1][0], rows.at[:, here]),
            (picked_image.at[mine], rhs_image.at[:, here]),
        )[kind]
        return remote(src, dst, ysend.at[kind, d - 1], yrecv.at[kind, d - 1], at(dy=d))

    for side in (0, 1):
        ocopy(side, 0, 1 - side).wait_recv()
        ocopy(side, 1, side).wait_recv()

    CHUNK = 64 * TILE

    def multiply(i, total):
        part = pl.ds(pl.multiple_of(i * CHUNK, CHUNK), CHUNK)
        return total + jnp.dot(lhs[:, part], omega_all[part], preferred_element_type=jnp.float32)

    total = lax.fori_loop(0, KMAX * TILE // CHUNK, multiply, jnp.zeros((TR * NS, TILE), jnp.float32))
    image = total.astype(BF)
    for r in range(TR):
        zbufs[1][0][r] = image[r * NS:(r + 1) * NS]

    def y_hook():
        for kind in (0, 1, 2):
            for d in (1, 3, 2):
                ycopy(kind, d).start()

    eye = lax.broadcasted_iota(jnp.int32, (TILE, TILE), 0) == lax.broadcasted_iota(
        jnp.int32, (TILE, TILE), 1
    )

    def early_hook():
        here = pl.ds(pl.multiple_of(y * NS, NS), NS)
        there = pl.ds(pl.multiple_of(NSAMP + y * NS, NS), NS)
        for r in range(TR):
            rows[r, here] = zbufs[1][0][r]
            rows[r, there] = zbufs[0][0][r]

        def keep(e, carry):
            rhs[e, here] = picked[y * SHARE + e]
            return carry

        lax.fori_loop(0, SHARE, keep, 0, unroll=8)
        for kind in (0, 1, 2):
            for d in range(1, NY):
                ycopy(kind, d).wait_recv()
        for r in range(TR):
            rows_t[r] = rows[r].T

        def start(e, carry):
            k = y * SHARE + e
            gradient = jnp.dot(rows_t[row_s[0, k], :, :NSAMP], rhs[e], preferred_element_type=jnp.float32)
            omega = omega_ref[e]
            on_diag = eye & (k < TR)
            inverse = jnp.where(on_diag, 1.0 / jnp.where(on_diag, omega, 1.0), 0.0)
            started[e] = omega - (gradient * (0.5 / NSAMP) - inverse)
            return carry

        lax.fori_loop(0, SHARE, start, 0, unroll=4)

    gather(1, (y_hook, lambda: None, lambda: None, early_hook))

    place = places[1]

    def image_own(k, carry):
        picked_image[k] = zbufs[1][0][k]
        return carry

    def image_other(k, carry):
        picked_image[k] = place[slot_s[0, k]]
        return carry

    lax.fori_loop(0, TR, image_own, 0, unroll=8)
    lax.fori_loop(TR, KMAX, image_other, 0, unroll=8)
    for d in (2, 1, 3):
        ycopy(3, d).start()

    def last(e, carry):
        rhs_image[e, pl.ds(pl.multiple_of(y * NS, NS), NS)] = picked_image[y * SHARE + e]
        return carry

    lax.fori_loop(0, SHARE, last, 0, unroll=8)
    for d in range(1, NY):
        ycopy(3, d).wait_recv()

    def update(e, carry):
        k = y * SHARE + e
        gradient = jnp.dot(rows_t[row_s[0, k], :, NSAMP:], rhs_image[e], preferred_element_type=jnp.float32)
        stepped = started[e] - gradient * (0.5 / NSAMP)
        shrunk = stepped - jnp.minimum(jnp.maximum(stepped, -penalty), penalty)
        proximal = jnp.where(eye & (k < TR), stepped, shrunk)
        held = jnp.where(active_s[0, k] > 0, proximal, omega_ref[e])
        out_ref[e] = jnp.where(k < count, held, 0.0)
        return carry

    lax.fori_loop(0, SHARE, update, 0, unroll=4)

    for phase in (0, 1):
        for j in range(1, CHUNKS):
            zcopy(phase, j).wait_send()
        wait_all(phase).wait_send()
    wplane().wait_send()
    for i in range(1, len(AROUND)):
        wforward(i).wait_send()
    for side in (0, 1):
        for half in (0, 1):
            ocopy(side, 0, half).wait_send()
        ocopy(side, 1, side).wait_send()
    for kind in range(4):
        for d in range(1, NY):
            ycopy(kind, d).wait_send()


def local(data, omega, tile_row, tile_col, tile_count, tile_active):
    vmem = pl.BlockSpec(memory_space=pltpu.VMEM)
    hbm = pl.BlockSpec(memory_space=pltpu.HBM)
    smem = pl.BlockSpec(memory_space=pltpu.SMEM)
    block = pltpu.VMEM((TR, NS, TILE), BF)
    scratch = [block] * (2 * CHUNKS)
    scratch += [pltpu.VMEM((SLOTS - LOCAL, NS, TILE), BF)] * 2
    scratch += [pltpu.VMEM((SLOTS, NS, TILE), BF)] * 2
    scratch += [pltpu.VMEM(data.shape, data.dtype), pltpu.VMEM(omega.shape, omega.dtype)]
    scratch += [
        pltpu.VMEM((KMAX * TILE, TILE), BF),
        pltpu.VMEM((TR * NS, KMAX * TILE), BF),
        pltpu.VMEM((KMAX, NS, TILE), BF),
        pltpu.VMEM((KMAX, NS, TILE), BF),
        pltpu.VMEM((SHARE, NSAMP, TILE), BF),
        pltpu.VMEM((SHARE, NSAMP, TILE), BF),
        pltpu.VMEM((SHARE, TILE, TILE), jnp.float32),
        pltpu.VMEM((TR, 2 * NSAMP, TILE), BF),
        pltpu.VMEM((TR, TILE, 2 * NSAMP), BF),
        pltpu.VMEM((len(AROUND) * PLANE, 1, TILE), jnp.int32),
        pltpu.SMEM((len(AROUND) * PLANE, 1, TILE), jnp.int32),
        pltpu.VMEM((1, KMAX), jnp.int32),
        pltpu.SMEM((1, KMAX), jnp.int32),
    ]
    dma = pltpu.SemaphoreType.DMA
    scratch += [dma((2, CHUNKS - 1)), dma((2, CHUNKS - 1)), dma((2,)), dma((2,))]
    scratch += [dma((len(AROUND),)), dma((len(AROUND),)), dma((4,))]
    scratch += [dma((6,)), dma((6,)), dma((4, NY - 1)), dma((4, NY - 1))]
    return pl.pallas_call(
        kernel,
        out_shape=jax.ShapeDtypeStruct(omega.shape, omega.dtype),
        in_specs=[hbm, hbm, vmem, smem, smem, smem, smem],
        out_specs=vmem,
        scratch_shapes=scratch,
        compiler_params=pltpu.CompilerParams(
            collective_id=0, has_side_effects=True, vmem_limit_bytes=32 * 2**20
        ),
    )(data, omega, tile_col, tile_row, tile_col, tile_count, tile_active)


def solution(mesh):
    placed = (
        P("samp", "var"),
        P(("var", "samp"), None, None),
        P("var", None),
        P("var", None),
        P("var"),
        P("var", None),
    )
    return jax.shard_map(
        local, mesh=mesh, in_specs=placed, out_specs=P(("var", "samp"), None, None), check_vma=False
    )
```

time: 82.5 us -> 75 us (0.909)
  Pallas kernels: 79.4 us -> 71 us
    pallas_call x1, Pallas kernels: 79.4 us -> 71 us  [local(): pl.pallas_call(kernel, out_shape=jax.ShapeDtypeStruct(omega.shape, omega....]
    unnamed x1 -> x11, local copies, waits for them, and re-layouts: 2.3 us -> 3.04 us
where the time goes in v3:
time: 75 us; the launch traced here: 74.8 us
  Pallas kernels  71 us (95%)
  local copies, waits for them, and re-layouts  3.04 us (4%)
    pallas_call x1, Pallas kernels, local(): pl.pallas_call(kernel, out_shape=jax.ShapeDtypeStruct(omega.shape, omega....  71 us
    unnamed x11, local copies, waits for them, and re-layouts  3.04 us

profile of v3, /device:TPU:1, one launch (start us, length us, event | category | flops | bytes accessed | tf_op | source)
XLA Modules:
  0.0 74.8 jit_solution(12962510321575524287)
XLA Ops:
  0.0 0.0 copy-start.4
  0.0 0.0 copy-start.2
  0.0 0.0 copy-start.3
  0.7 0.0 copy-done.4
  0.7 0.0 copy-done.2
  0.7 0.0 copy-done.3
  0.7 0.0 copy-start
  0.7 1.2 %copy-done = f32[16,128,128]{2,1,0:T(8,128)S(1)} copy-done((f32[16,128,128]{2,1,0:T(8,128)S(1)}, f32[16,128,128]{2,1,0:T(8,128)}, u32[]{:S(2)}) %copy-start) | copy-done | bytes 1048600
  2.0 0.0 copy-start.1
  2.0 0.8 %copy-done.1 = bf16[32,1024]{1,0:T(8,128)(2,1)S(1)} copy-done((bf16[32,1024]{1,0:T(8,128)(2,1)S(1)}, bf16[32,1024]{1,0:T(8,128)(2,1)}, u32[]{:S(2)}) %copy-start.1) | copy-done | bytes 65560
  2.8 71.0 %shard_map.64 = f32[16,128,128]{2,1,0:T(8,128)S(1)} custom-call(bf16[32,1024]{1,0:T(8,128)(2,1)S(1)} %copy-done.1, f32[16,128,128]{2,1,0:T(8,128)S(1)} %copy-done, s32[1,64]{1,0:T(1,128)S(1)} %copy-done.2, s32[1,64]{1,0:T(1,128)S(1)} %copy-done.3, s32[1,64]{1,0:T(1,128)S(1)} %copy-done.2, s32[1]{0:T(128)S(6)} %copy.8.count_s, s32[1,64]{1,0:T(1,128)S(1)} %copy-done.4), custom_call_target="tpu_custom_call" | custom-call | tf_op jit(solution)/shard_map/pallas_call | solution.py:429
  73.8 1.0 %copy.9 = f32[16,128,128]{2,1,0:T(8,128)} copy(f32[16,128,128]{2,1,0:T(8,128)S(1)} %shard_map.64) | data formatting | bytes 2097152
Async XLA Ops:
  0.0 0.7 copy-start.4
  0.0 0.7 copy-start.2
  0.0 0.7 copy-start.3
  0.7 1.2 %copy-start = (f32[16,128,128]{2,1,0:T(8,128)S(1)}, f32[16,128,128]{2,1,0:T(8,128)}, u32[]{:S(2)}) copy-start(f32[16,128,128]{2,1,0:T(8,128)} %omega_hbm.1) | copy-start | bytes 3145732
  2.0 0.8 %copy-start.1 = (bf16[32,1024]{1,0:T(8,128)(2,1)S(1)}, bf16[32,1024]{1,0:T(8,128)(2,1)}, u32[]{:S(2)}) copy-start(bf16[32,1024]{1,0:T(8,128)(2,1)} %data_hbm.1) | copy-start | bytes 196612

commit v4 on v3

--- a/solution.py
+++ b/solution.py
@@ -39,6 +39,13 @@
     return (((NX - dx) % NX) * NC + dc) * STRIDE + (STRIDE - i) % STRIDE
 
 
+def links(g):
+    dx, dz, dc = split(g)
+    return 2 * min(dx, NX - dx) + min(dz, NZ - dz)
+
+
+FAR_FIRST = sorted(range(1, GROUPS), key=lambda g: -links(g))
+
 AROUND = (0, 1, NZ - 1, 2, NZ - 2)
 
 
@@ -61,7 +68,7 @@
     want_v, want_s, slot_v, slot_s = take(4)
     zsend, zrecv, xsend, xrecv = take(4)
     wsend, wrecv, lsem = take(3)
-    osend, orecv, ysend, yrecv = take(4)
+    osend, orecv, ysend, yrecv, lsend, lrecv = take(6)
 
     load_data = pltpu.make_async_copy(data_hbm, data_ref, lsem.at[2])
     load_omega = pltpu.make_async_copy(omega_hbm, omega_ref, lsem.at[3])
@@ -121,11 +128,12 @@
     side = jnp.where(side == 0, 2, side - 1)
     far = jnp.where(far == 2, 0, jnp.where(far == 3, 1, jnp.where(far == 1, 2, jnp.where(far == 4, 3, 4))))
     plane = dx * NC + dc
-    slot_v[...] = jnp.where(
+    entry = lax.broadcasted_iota(jnp.int32, cols.shape, 1)
+    slot_v[...] = jnp.where(entry < TR, SLOTS + entry, jnp.where(
         opposite,
         GROUPS * CHUNKS + plane,
         (plane * STRIDE + side) * CHUNKS + far,
-    )
+    ))
 
     load_data.wait()
     for t in range(TR):
@@ -169,10 +177,13 @@
             for g in range(GROUPS, GROUPS + PLANE):
                 base = GROUPS * CHUNKS - GROUPS
                 send(g, base + g - LOCAL, base + mirrored(g), (3,) if g % NC else (4,))
-        for g in range(1, GROUPS):
+        for g in FAR_FIRST:
             send(g, g * CHUNKS + first - LOCAL, mirrored(g) * CHUNKS + first, pieces)
         for j in pieces:
             place[j] = tile(0, j)
+        if first == 3:
+            for t in range(TR):
+                place[SLOTS + t] = bufs[0][t]
 
     def gather(phase, hooks):
         zcopy(phase, 1).start()
@@ -288,7 +299,7 @@
             (picked.at[mine], rhs.at[:, here]),
             (zbufs[0][0], rows.at[:, there]),
             (zbufs[1][0], rows.at[:, here]),
-            (picked_image.at[mine], rhs_image.at[:, here]),
+            (None, None),
         )[kind]
         return remote(src, dst, ysend.at[kind, d - 1], yrecv.at[kind, d - 1], at(dy=d))
 
@@ -345,30 +356,33 @@
 
         lax.fori_loop(0, SHARE, start, 0, unroll=4)
 
-    gather(1, (y_hook, lambda: None, lambda: None, early_hook))
+    gather(1, (lambda: None, y_hook, lambda: None, early_hook))
 
     place = places[1]
 
-    def image_own(k, carry):
-        picked_image[k] = zbufs[1][0][k]
-        return carry
-
-    def image_other(k, carry):
-        picked_image[k] = place[slot_s[0, k]]
-        return carry
-
-    lax.fori_loop(0, TR, image_own, 0, unroll=8)
-    lax.fori_loop(TR, KMAX, image_other, 0, unroll=8)
-    for d in (2, 1, 3):
-        ycopy(3, d).start()
-
-    def last(e, carry):
-        rhs_image[e, pl.ds(pl.multiple_of(y * NS, NS), NS)] = picked_image[y * SHARE + e]
-        return carry
-
-    lax.fori_loop(0, SHARE, last, 0, unroll=8)
-    for d in range(1, NY):
-        ycopy(3, d).wait_recv()
+    PART = SHARE // 2
+
+    def lastcopy(d, half):
+        here = pl.ds(pl.multiple_of(y * NS, NS), NS)
+        return remote(
+            picked_image.at[pl.ds(ys[d] * SHARE + half * PART, PART)],
+            rhs_image.at[pl.ds(half * PART, PART), here],
+            lsend.at[half, d - 1],
+            lrecv.at[half, d - 1],
+            at(dy=d),
+        )
+
+    for half in (0, 1):
+        for d in (2, 1, 3, 0):
+            for e in range(half * PART, (half + 1) * PART):
+                k = ys[d] * SHARE + e
+                tile = place[slot_s[0, k]]
+                if d:
+                    picked_image[k] = tile
+                else:
+                    rhs_image[e, pl.ds(pl.multiple_of(y * NS, NS), NS)] = tile
+            if d:
+                lastcopy(d, half).start()
 
     def update(e, carry):
         k = y * SHARE + e
@@ -380,7 +394,10 @@
         out_ref[e] = jnp.where(k < count, held, 0.0)
         return carry
 
-    lax.fori_loop(0, SHARE, update, 0, unroll=4)
+    for half in (0, 1):
+        for d in range(1, NY):
+            lastcopy(d, half).wait_recv()
+        lax.fori_loop(half * PART, (half + 1) * PART, update, 0, unroll=4)
 
     for phase in (0, 1):
         for j in range(1, CHUNKS):
@@ -393,9 +410,11 @@
         for half in (0, 1):
             ocopy(side, 0, half).wait_send()
         ocopy(side, 1, side).wait_send()
-    for kind in range(4):
-        for d in range(1, NY):
+    for d in range(1, NY):
+        for kind in range(3):
             ycopy(kind, d).wait_send()
+        for half in (0, 1):
+            lastcopy(d, half).wait_send()
 
 
 def local(data, omega, tile_row, tile_col, tile_count, tile_active):
@@ -405,7 +424,7 @@
     block = pltpu.VMEM((TR, NS, TILE), BF)
     scratch = [block] * (2 * CHUNKS)
     scratch += [pltpu.VMEM((SLOTS - LOCAL, NS, TILE), BF)] * 2
-    scratch += [pltpu.VMEM((SLOTS, NS, TILE), BF)] * 2
+    scratch += [pltpu.VMEM((SLOTS + TR, NS, TILE), BF)] * 2
     scratch += [pltpu.VMEM(data.shape, data.dtype), pltpu.VMEM(omega.shape, omega.dtype)]
     scratch += [
         pltpu.VMEM((KMAX * TILE, TILE), BF),
@@ -425,7 +444,7 @@
     dma = pltpu.SemaphoreType.DMA
     scratch += [dma((2, CHUNKS - 1)), dma((2, CHUNKS - 1)), dma((2,)), dma((2,))]
     scratch += [dma((len(AROUND),)), dma((len(AROUND),)), dma((4,))]
-    scratch += [dma((6,)), dma((6,)), dma((4, NY - 1)), dma((4, NY - 1))]
+    scratch += [dma((6,)), dma((6,)), dma((3, NY - 1)), dma((3, NY - 1)), dma((2, NY - 1)), dma((2, NY - 1))]
     return pl.pallas_call(
         kernel,
         out_shape=jax.ShapeDtypeStruct(omega.shape, omega.dtype),

time: 75 us -> 72.6 us (0.968)
  Pallas kernels: 71 us -> 68.6 us
    pallas_call x1, Pallas kernels: 71 us -> 68.6 us  [local(): pl.pallas_call(kernel, out_shape=jax.ShapeDtypeStruct(omega.shape, omega....]
where the time goes in v4:
time: 72.6 us; the launch traced here: 72.4 us
  Pallas kernels  68.6 us (94%)
  local copies, waits for them, and re-layouts  3.04 us (4%)
  between operations  0.74 us (1%)
    pallas_call x1, Pallas kernels, local(): pl.pallas_call(kernel, out_shape=jax.ShapeDtypeStruct(omega.shape, omega....  68.6 us
    unnamed x11, local copies, waits for them, and re-layouts  3.04 us

profile of v4, /device:TPU:1, one launch (start us, length us, event | category | flops | bytes accessed | tf_op | source)
XLA Modules:
  0.0 72.4 jit_solution(12711154561509744610)
XLA Ops:
  0.0 0.0 copy-start.4
  0.0 0.0 copy-start.2
  0.0 0.0 copy-start.3
  0.7 0.0 copy-done.4
  0.7 0.0 copy-done.2
  0.7 0.0 copy-done.3
  0.7 0.0 copy-start
  0.7 1.2 %copy-done = f32[16,128,128]{2,1,0:T(8,128)S(1)} copy-done((f32[16,128,128]{2,1,0:T(8,128)S(1)}, f32[16,128,128]{2,1,0:T(8,128)}, u32[]{:S(2)}) %copy-start) | copy-done | bytes 1048600
  2.0 0.0 copy-start.1
  2.0 0.8 %copy-done.1 = bf16[32,1024]{1,0:T(8,128)(2,1)S(1)} copy-done((bf16[32,1024]{1,0:T(8,128)(2,1)S(1)}, bf16[32,1024]{1,0:T(8,128)(2,1)}, u32[]{:S(2)}) %copy-start.1) | copy-done | bytes 65560
  2.8 68.6 %shard_map.64 = f32[16,128,128]{2,1,0:T(8,128)S(1)} custom-call(bf16[32,1024]{1,0:T(8,128)(2,1)S(1)} %copy-done.1, f32[16,128,128]{2,1,0:T(8,128)S(1)} %copy-done, s32[1,64]{1,0:T(1,128)S(1)} %copy-done.2, s32[1,64]{1,0:T(1,128)S(1)} %copy-done.3, s32[1,64]{1,0:T(1,128)S(1)} %copy-done.2, s32[1]{0:T(128)S(6)} %copy.8.count_s, s32[1,64]{1,0:T(1,128)S(1)} %copy-done.4), custom_call_target="tpu_custom_call" | custom-call | tf_op jit(solution)/shard_map/pallas_call | solution.py:448
  71.4 1.0 %copy.9 = f32[16,128,128]{2,1,0:T(8,128)} copy(f32[16,128,128]{2,1,0:T(8,128)S(1)} %shard_map.64) | data formatting | bytes 2097152
Async XLA Ops:
  0.0 0.7 copy-start.4
  0.0 0.7 copy-start.2
  0.0 0.7 copy-start.3
  0.7 1.2 %copy-start = (f32[16,128,128]{2,1,0:T(8,128)S(1)}, f32[16,128,128]{2,1,0:T(8,128)}, u32[]{:S(2)}) copy-start(f32[16,128,128]{2,1,0:T(8,128)} %omega_hbm.1) | copy-start | bytes 3145732
  2.0 0.8 %copy-start.1 = (bf16[32,1024]{1,0:T(8,128)(2,1)S(1)}, bf16[32,1024]{1,0:T(8,128)(2,1)}, u32[]{:S(2)}) copy-start(bf16[32,1024]{1,0:T(8,128)(2,1)} %data_hbm.1) | copy-start | bytes 196612

commit v5 on v4

--- a/solution.py
+++ b/solution.py
@@ -50,7 +50,7 @@
 
 
 def kernel(
-    data_hbm, omega_hbm, cols_ref, row_s, col_s, count_s, active_s, out_ref,
+    data_hbm, omega_hbm, cols_ref, row_s, col_s, count_s, active_s, out_hbm,
     *scratch,
 ):
     scratch = list(scratch)
@@ -63,7 +63,7 @@
     zbufs = [take(CHUNKS), take(CHUNKS)]
     stages = take(2)
     places = take(2)
-    data_ref, omega_ref = take(2)
+    data_ref, omega_ref, out_ref = take(3)
     omega_all, lhs, picked, picked_image, rhs, rhs_image, started, rows, rows_t = take(9)
     want_v, want_s, slot_v, slot_s = take(4)
     zsend, zrecv, xsend, xrecv = take(4)
@@ -360,7 +360,7 @@
 
     place = places[1]
 
-    PART = SHARE // 2
+    PART = SHARE // 4
 
     def lastcopy(d, half):
         here = pl.ds(pl.multiple_of(y * NS, NS), NS)
@@ -372,7 +372,7 @@
             at(dy=d),
         )
 
-    for half in (0, 1):
+    for half in range(4):
         for d in (2, 1, 3, 0):
             for e in range(half * PART, (half + 1) * PART):
                 k = ys[d] * SHARE + e
@@ -394,10 +394,15 @@
         out_ref[e] = jnp.where(k < count, held, 0.0)
         return carry
 
-    for half in (0, 1):
+    def outcopy(half):
+        part = pl.ds(half * PART, PART)
+        return pltpu.make_async_copy(out_ref.at[part], out_hbm.at[part], lsem.at[2 + half])
+
+    for half in range(4):
         for d in range(1, NY):
             lastcopy(d, half).wait_recv()
         lax.fori_loop(half * PART, (half + 1) * PART, update, 0, unroll=4)
+        outcopy(half).start()
 
     for phase in (0, 1):
         for j in range(1, CHUNKS):
@@ -413,8 +418,10 @@
     for d in range(1, NY):
         for kind in range(3):
             ycopy(kind, d).wait_send()
-        for half in (0, 1):
+        for half in range(4):
             lastcopy(d, half).wait_send()
+    for half in range(4):
+        outcopy(half).wait()
 
 
 def local(data, omega, tile_row, tile_col, tile_count, tile_active):
@@ -425,7 +432,7 @@
     scratch = [block] * (2 * CHUNKS)
     scratch += [pltpu.VMEM((SLOTS - LOCAL, NS, TILE), BF)] * 2
     scratch += [pltpu.VMEM((SLOTS + TR, NS, TILE), BF)] * 2
-    scratch += [pltpu.VMEM(data.shape, data.dtype), pltpu.VMEM(omega.shape, omega.dtype)]
+    scratch += [pltpu.VMEM(data.shape, data.dtype), pltpu.VMEM(omega.shape, omega.dtype)] + [pltpu.VMEM(omega.shape, omega.dtype)]
     scratch += [
         pltpu.VMEM((KMAX * TILE, TILE), BF),
         pltpu.VMEM((TR * NS, KMAX * TILE), BF),
@@ -443,16 +450,16 @@
     ]
     dma = pltpu.SemaphoreType.DMA
     scratch += [dma((2, CHUNKS - 1)), dma((2, CHUNKS - 1)), dma((2,)), dma((2,))]
-    scratch += [dma((len(AROUND),)), dma((len(AROUND),)), dma((4,))]
-    scratch += [dma((6,)), dma((6,)), dma((3, NY - 1)), dma((3, NY - 1)), dma((2, NY - 1)), dma((2, NY - 1))]
+    scratch += [dma((len(AROUND),)), dma((len(AROUND),)), dma((6,))]
+    scratch += [dma((6,)), dma((6,)), dma((3, NY - 1)), dma((3, NY - 1)), dma((4, NY - 1)), dma((4, NY - 1))]
     return pl.pallas_call(
         kernel,
         out_shape=jax.ShapeDtypeStruct(omega.shape, omega.dtype),
         in_specs=[hbm, hbm, vmem, smem, smem, smem, smem],
-        out_specs=vmem,
+        out_specs=hbm,
         scratch_shapes=scratch,
         compiler_params=pltpu.CompilerParams(
-            collective_id=0, has_side_effects=True, vmem_limit_bytes=32 * 2**20
+            collective_id=0, has_side_effects=True, vmem_limit_bytes=60 * 2**20
         ),
     )(data, omega, tile_col, tile_row, tile_col, tile_count, tile_active)
 

time: 72.6 us -> 72.4 us (level)
  local copies, waits for them, and re-layouts: 3.04 us -> 2.3 us
    unnamed x11 -> x1, local copies, waits for them, and re-layouts: 3.04 us -> 2.3 us
where the time goes in v5:
time: 72.4 us; the launch traced here: 72.2 us
  Pallas kernels  69.3 us (96%)
  local copies, waits for them, and re-layouts  2.3 us (3%)
    pallas_call x1, Pallas kernels, local(): pl.pallas_call(kernel, out_shape=jax.ShapeDtypeStruct(omega.shape, omega....  69.3 us
    unnamed x1, local copies, waits for them, and re-layouts  2.3 us

profile of v5, /device:TPU:1, one launch (start us, length us, event | category | flops | bytes accessed | tf_op | source)
XLA Modules:
  0.0 72.2 jit_solution(12396569338107453918)
XLA Ops:
  0.7 69.3 %shard_map.64 = f32[16,128,128]{2,1,0:T(8,128)} custom-call(bf16[32,1024]{1,0:T(8,128)(2,1)} %data_hbm.1, f32[16,128,128]{2,1,0:T(8,128)} %omega_hbm.1, s32[1,64]{1,0:T(1,128)} %col_s.1, s32[1,64]{1,0:T(1,128)} %row_s.1, s32[1,64]{1,0:T(1,128)} %col_s.1, s32[1]{0:T(128)S(6)} %copy.8.count_s, s32[1,64]{1,0:T(1,128)} %active_s.1), custom_call_target="tpu_custom_call" | custom-call | tf_op jit(solution)/shard_map/pallas_call | solution.py:455
  69.9 2.3 %copy.9 = f32[16,128,128]{2,1,0:T(8,128)} copy(f32[16,128,128]{2,1,0:T(8,128)} %shard_map.64) | data formatting | bytes 2097152
